TPU v7x, 32 devices: a whole 2x2x4 slice. The times are simulated.
32 devices in a mesh: group: 16 (over z, x, core), dp: 2 (over y).
Axes of the slice: x: 2, y: 2, z: 4, core: 2. Of those that a mesh axis runs over, the one named last changes fastest.
Arguments:
- frames: bfloat16 [32768, 768], P(('group', 'dp')), may hold values from -6 to 6
- lengths: int32 [32, 2], P(('group', 'dp')), may hold values from 0 to 1024, as said below
- mask_starts: int32 [32768], P(('group', 'dp')), may hold values 0 or 1
- width_code: int32 [16], P('group'), may hold values from 0 to 2
- head_code: int32 [16], P('group'), may hold values from 0 to 4
- ffn_code: int32 [16], P('group'), may hold values from 0 to 2
- qkv_weight: float32 [768, 2304], P('group'), may hold values from -0.3125 to 0.3125
- out_weight: float32 [768, 768], P('group'), may hold values from -0.625 to 0.625
- ffn_in_weight: float32 [768, 3072], P('group'), may hold values from -0.21875 to 0.21875
- ffn_out_weight: float32 [3072, 768], P('group'), may hold values from -0.109375 to 0.109375
- ffn_bias: float32 [3072, 1], P('group'), may hold values from -3 to 3
- norm_gains: float32 [768, 2], P('group'), may hold values from 0.1 to 1.9
- shifts: float32 [768, 7], P('group'), may hold values from -3 to 3
- cotangent: bfloat16 [32768, 768], P(('group', 'dp')), may hold values from -6 to 6
Outputs:
- layer_out: bfloat16 [32768, 768], P(('group', 'dp'))
- frames_grad: float32 [32768, 768], P(('group', 'dp'))
- qkv_grad: float32 [768, 2304], P('group')
- out_grad: float32 [768, 768], P('group')
- ffn_in_grad: float32 [768, 3072], P('group')
- ffn_out_grad: float32 [3072, 768], P('group')
- ffn_bias_grad: float32 [3072, 1], P('group')
- gains_grad: float32 [768, 2], P('group')
- shifts_grad: float32 [768, 7], P('group')
Inputs may be any that keep to these rules, and one draw needn't show every extreme that they name: `lengths`: per device: the first utterance has 300 to 1024 frames, the second is 0 (absent) or 300 or more, together at most 1024; some device holds one utterance of exactly 1024 frames.
All inputs are finite; a program needn't handle non-finite values. No bound on the sum of `mask_starts` on one device may be relied on, other than what follows from the above.
Results may differ from a plain program's by a relative error of at most 0.015.
The roundings to bfloat16 on the way count: a program that leaves them out, or rounds other values in their place, can miss the bound.
Values may be sent and summed in bfloat16 or wider, within the bound.
A program may use at most 192 MiB of HBM per device.

v0:
```python
import jax
import jax.numpy as jnp
from jax import lax
from jax.sharding import PartitionSpec as P

D = 768
HEADS = 12
FF = 3072
FRAMES = 1024
SPAN = 10
UTT_DEV = 2


norm_eps = 1e-05
far_score = -1000000000.0
root_half = 0.7071067811865476
inv_root_tau = 0.3989422804014327


def subnet_masks(width_pick, head_pick, ffn_pick):
    sub_width = D * (4 + width_pick) // 6
    head_count = HEADS - HEADS // 3 + head_pick
    ffn_width = sub_width * (6 + ffn_pick) // 2
    feature_mask = (jnp.arange(D, dtype=jnp.int32) < sub_width).astype(jnp.float32)
    head_mask = (jnp.arange(D, dtype=jnp.int32) < head_count * (D // HEADS)).astype(jnp.float32)
    ffn_mask = (jnp.arange(FF, dtype=jnp.int32) < ffn_width).astype(jnp.float32)
    return (feature_mask, head_mask, ffn_mask, sub_width.astype(jnp.float32))


def frame_layout(block_lengths, starts):
    places = jnp.arange(FRAMES, dtype=jnp.int32)
    bounds = jnp.cumsum(block_lengths)
    segment = jnp.sum((places[:, None] >= bounds[None, :]).astype(jnp.int32), axis=1)
    live_rows = (segment < UTT_DEV).astype(jnp.int32)
    hit_count = jnp.zeros((FRAMES,), jnp.int32)
    for offset in range(SPAN):
        earlier = jnp.concatenate([jnp.zeros((offset,), jnp.int32), starts[: FRAMES - offset]])
        earlier_seg = jnp.concatenate(
            [jnp.full((offset,), -1, jnp.int32), segment[: FRAMES - offset]]
        )
        hit_count = jnp.maximum(
            hit_count, ((earlier == 1) & (earlier_seg == segment)).astype(jnp.int32)
        )
    masked = hit_count * live_rows
    return (segment, live_rows.astype(jnp.float32), masked.astype(jnp.float32))


def norm_forward(residual, gain_vec, shift_vec, feature_mask, sub_width):
    center = jnp.sum(residual, axis=1, keepdims=True) / sub_width
    centered = (residual - center) * feature_mask
    variance = jnp.sum(centered * centered, axis=1, keepdims=True) / sub_width
    inv_std = lax.rsqrt(variance + norm_eps)
    normed = centered * inv_std
    return (normed * gain_vec * feature_mask + shift_vec * feature_mask, normed, inv_std)


def norm_backward(grad_out, gain_vec, normed, inv_std, feature_mask, sub_width):
    grad_normed = grad_out * gain_vec * feature_mask
    mean_grad = jnp.sum(grad_normed, axis=1, keepdims=True) / sub_width
    mean_cross = jnp.sum(grad_normed * normed, axis=1, keepdims=True) / sub_width
    grad_in = inv_std * (grad_normed - mean_grad - normed * mean_cross) * feature_mask
    return (grad_in, jnp.sum(grad_out * normed, axis=0), jnp.sum(grad_out, axis=0) * feature_mask)


def gelu_slope(pre_act):
    return (
        0.5 * (1.0 + lax.erf(pre_act * root_half))
        + pre_act * jnp.exp(-0.5 * pre_act * pre_act) * inv_root_tau
    )


def column_block(matrix, col_start, col_count):
    return lax.dynamic_slice_in_dim(matrix, col_start, col_count, 1)


def on_device(
    frames,
    lengths,
    mask_starts,
    width_code,
    head_code,
    ffn_code,
    qkv_weight,
    out_weight,
    ffn_in_weight,
    ffn_out_weight,
    ffn_bias,
    norm_gains,
    shifts,
    cotangent,
):
    feature_mask, head_mask, ffn_mask, sub_width = subnet_masks(
        width_code[0], head_code[0], ffn_code[0]
    )
    segment, live_rows, masked = frame_layout(lengths[0], mask_starts)
    same_seg = segment[:, None] == segment[None, :]
    frame_rows = frames.shape[0]
    head_dim = D // HEADS
    pair_width = 2 * head_dim
    score_scale = head_dim ** (-0.5)
    three_mask = jnp.concatenate([head_mask, head_mask, head_mask])

    def pair_scores(projected, col_start):
        query_heads = column_block(projected, col_start, pair_width).reshape(
            frame_rows, 2, head_dim
        )
        key_heads = column_block(projected, D + col_start, pair_width).reshape(
            frame_rows, 2, head_dim
        )
        value_heads = column_block(projected, 2 * D + col_start, pair_width).reshape(
            frame_rows, 2, head_dim
        )
        scores = (
            jnp.einsum("qhd,khd->hqk", query_heads, key_heads, preferred_element_type=jnp.float32)
            * score_scale
        )
        return (query_heads, key_heads, value_heads, jnp.where(same_seg[None], scores, far_score))

    def attention_part(qkv_full, out_full, gains_full, shifts_full):
        shift_table = shifts_full.astype(jnp.float32)
        start_vec = (
            jnp.where(masked[:, None] > 0, shift_table[:, 6][None, :], frames.astype(jnp.float32))
            * feature_mask
        )
        start_low = start_vec.astype(jnp.bfloat16)
        qkv_masked = qkv_full * (feature_mask[:, None] * three_mask[None, :]).astype(jnp.bfloat16)
        proj_bias = jnp.concatenate(
            [
                shift_table[:, 0] * head_mask,
                jnp.zeros((D,), jnp.float32),
                shift_table[:, 1] * head_mask,
            ]
        )
        projected = (
            jnp.dot(start_low, qkv_masked, preferred_element_type=jnp.float32) + proj_bias
        ).astype(jnp.bfloat16)

        def pair_forward(pair_index, loop_state):
            mixed_buf, lse_buf = loop_state
            col_start = pair_index * pair_width
            query_heads, key_heads, value_heads, scores = pair_scores(projected, col_start)
            row_peak = jnp.max(scores, axis=2, keepdims=True)
            weights = jnp.exp(scores - row_peak)
            denominator = jnp.sum(weights, axis=2, keepdims=True)
            weights_low = (weights / denominator).astype(jnp.bfloat16)
            pair_mixed = jnp.einsum(
                "hqk,khd->qhd", weights_low, value_heads, preferred_element_type=jnp.float32
            )
            mixed_buf = lax.dynamic_update_slice(
                mixed_buf,
                pair_mixed.reshape(frame_rows, pair_width).astype(jnp.bfloat16),
                (0, col_start),
            )
            lse_buf = lax.dynamic_update_slice(
                lse_buf, (row_peak + jnp.log(denominator))[:, :, 0], (2 * pair_index, 0)
            )
            return (mixed_buf, lse_buf)

        mixed_low, lse_buf = lax.fori_loop(
            0,
            HEADS // 2,
            pair_forward,
            (jnp.zeros((frame_rows, D), jnp.bfloat16), jnp.zeros((HEADS, frame_rows), jnp.float32)),
        )
        out_masked = out_full * (head_mask[:, None] * feature_mask[None, :]).astype(jnp.bfloat16)
        branch = (
            jnp.dot(mixed_low, out_masked, preferred_element_type=jnp.float32)
            + shift_table[:, 2] * feature_mask
        )
        gains_table = gains_full.astype(jnp.float32)
        hidden_one, normed_one, inv_one = norm_forward(
            start_vec + branch, gains_table[:, 0], shift_table[:, 4], feature_mask, sub_width
        )
        return (
            start_low,
            qkv_masked,
            projected,
            mixed_low,
            lse_buf,
            out_masked,
            hidden_one,
            normed_one,
            inv_one,
        )

    qkv_full, out_full, ffn_in_full, ffn_out_full, ffn_bias_full, gains_full, shifts_full = (
        lax.all_gather(qkv_weight.astype(jnp.bfloat16), "group", axis=0, tiled=True),
        lax.all_gather(out_weight.astype(jnp.bfloat16), "group", axis=0, tiled=True),
        lax.all_gather(ffn_in_weight.astype(jnp.bfloat16), "group", axis=0, tiled=True),
        lax.all_gather(ffn_out_weight.astype(jnp.bfloat16), "group", axis=0, tiled=True),
        lax.all_gather(ffn_bias.astype(jnp.bfloat16), "group", axis=0, tiled=True),
        lax.all_gather(norm_gains.astype(jnp.bfloat16), "group", axis=0, tiled=True),
        lax.all_gather(shifts.astype(jnp.bfloat16), "group", axis=0, tiled=True),
    )
    front_state = attention_part(qkv_full, out_full, gains_full, shifts_full)
    (
        start_low,
        qkv_masked,
        projected,
        mixed_low,
        lse_buf,
        out_masked,
        hidden_one,
        normed_one,
        inv_one,
    ) = front_state
    shift_table = shifts_full.astype(jnp.float32)
    gains_table = gains_full.astype(jnp.float32)
    hidden_low = hidden_one.astype(jnp.bfloat16)
    in_masked = ffn_in_full * (feature_mask[:, None] * ffn_mask[None, :]).astype(jnp.bfloat16)
    pre_act = (
        jnp.dot(hidden_low, in_masked, preferred_element_type=jnp.float32)
        + ffn_bias_full[:, 0].astype(jnp.float32) * ffn_mask
    )
    act_low = jax.nn.gelu(pre_act, approximate=False).astype(jnp.bfloat16)
    down_masked = ffn_out_full * (ffn_mask[:, None] * feature_mask[None, :]).astype(jnp.bfloat16)
    ffn_branch = (
        jnp.dot(act_low, down_masked, preferred_element_type=jnp.float32)
        + shift_table[:, 3] * feature_mask
    )
    result, normed_two, inv_two = norm_forward(
        hidden_one + ffn_branch, gains_table[:, 1], shift_table[:, 5], feature_mask, sub_width
    )
    layer_out = (result * live_rows[:, None]).astype(jnp.bfloat16)
    grad_result = cotangent.astype(jnp.float32) * live_rows[:, None]
    grad_two, gain_two, shift_two = norm_backward(
        grad_result, gains_table[:, 1], normed_two, inv_two, feature_mask, sub_width
    )
    grad_ffn = grad_two.astype(jnp.bfloat16)
    ffn_out_part = jnp.einsum("tf,td->fd", act_low, grad_ffn, preferred_element_type=jnp.float32)
    grad_act = jnp.einsum("td,fd->tf", grad_ffn, down_masked, preferred_element_type=jnp.float32)
    grad_pre = (grad_act * gelu_slope(pre_act)).astype(jnp.bfloat16)
    ffn_in_part = jnp.einsum("td,tf->df", hidden_low, grad_pre, preferred_element_type=jnp.float32)
    grad_hidden = (
        jnp.einsum("tf,df->td", grad_pre, in_masked, preferred_element_type=jnp.float32) + grad_two
    )
    grad_one, gain_one, shift_one = norm_backward(
        grad_hidden, gains_table[:, 0], normed_one, inv_one, feature_mask, sub_width
    )
    grad_branch = grad_one.astype(jnp.bfloat16)
    out_part = jnp.einsum("ta,td->ad", mixed_low, grad_branch, preferred_element_type=jnp.float32)
    grad_mixed = jnp.einsum(
        "td,ad->ta", grad_branch, out_masked, preferred_element_type=jnp.float32
    ).astype(jnp.bfloat16)

    def pair_backward(pair_index, grad_proj):
        col_start = pair_index * pair_width
        query_heads, key_heads, value_heads, scores = pair_scores(projected, col_start)
        grad_heads = column_block(grad_mixed, col_start, pair_width).reshape(
            frame_rows, 2, head_dim
        )
        pair_lse = lax.dynamic_slice_in_dim(lse_buf, 2 * pair_index, 2, 0)
        probs = jnp.exp(scores - pair_lse[:, :, None])
        grad_values = jnp.einsum(
            "hqk,qhd->khd",
            probs.astype(jnp.bfloat16),
            grad_heads,
            preferred_element_type=jnp.float32,
        )
        grad_probs = jnp.einsum(
            "qhd,khd->hqk", grad_heads, value_heads, preferred_element_type=jnp.float32
        )
        row_inner = jnp.sum(probs * grad_probs, axis=2, keepdims=True)
        grad_scores = (probs * (grad_probs - row_inner)).astype(jnp.bfloat16)
        grad_queries = (
            jnp.einsum("hqk,khd->qhd", grad_scores, key_heads, preferred_element_type=jnp.float32)
            * score_scale
        )
        grad_keys = (
            jnp.einsum("hqk,qhd->khd", grad_scores, query_heads, preferred_element_type=jnp.float32)
            * score_scale
        )
        grad_proj = lax.dynamic_update_slice(
            grad_proj,
            grad_queries.reshape(frame_rows, pair_width).astype(jnp.bfloat16),
            (0, col_start),
        )
        grad_proj = lax.dynamic_update_slice(
            grad_proj,
            grad_keys.reshape(frame_rows, pair_width).astype(jnp.bfloat16),
            (0, D + col_start),
        )
        grad_proj = lax.dynamic_update_slice(
            grad_proj,
            grad_values.reshape(frame_rows, pair_width).astype(jnp.bfloat16),
            (0, 2 * D + col_start),
        )
        return grad_proj

    grad_proj = lax.fori_loop(
        0, HEADS // 2, pair_backward, jnp.zeros((frame_rows, 3 * D), jnp.bfloat16)
    )
    qkv_part = jnp.einsum("td,tc->dc", start_low, grad_proj, preferred_element_type=jnp.float32)
    grad_start = (
        jnp.einsum("tc,dc->td", grad_proj, qkv_masked, preferred_element_type=jnp.float32)
        + grad_one
    )
    frames_grad = grad_start * (1.0 - masked[:, None])
    proj_sums = jnp.sum(grad_proj, axis=0, dtype=jnp.float32)
    shifts_part = jnp.stack(
        [
            proj_sums[:D],
            proj_sums[2 * D :],
            jnp.sum(grad_branch, axis=0, dtype=jnp.float32),
            jnp.sum(grad_ffn, axis=0, dtype=jnp.float32),
            shift_one,
            shift_two,
            jnp.sum(grad_start * masked[:, None], axis=0),
        ],
        axis=1,
    )
    gains_part = jnp.stack([gain_one, gain_two], axis=1)
    ffn_bias_part = jnp.sum(grad_pre, axis=0, dtype=jnp.float32)[:, None]
    qkv_own, out_own, ffn_in_own, ffn_out_own, bias_own, gains_own, shifts_own = (
        lax.psum_scatter(qkv_part, "group", scatter_dimension=0, tiled=True),
        lax.psum_scatter(out_part, "group", scatter_dimension=0, tiled=True),
        lax.psum_scatter(ffn_in_part, "group", scatter_dimension=0, tiled=True),
        lax.psum_scatter(ffn_out_part, "group", scatter_dimension=0, tiled=True),
        lax.psum_scatter(ffn_bias_part, "group", scatter_dimension=0, tiled=True),
        lax.psum_scatter(gains_part, "group", scatter_dimension=0, tiled=True),
        lax.psum_scatter(shifts_part, "group", scatter_dimension=0, tiled=True),
    )
    qkv_grad, out_grad, ffn_in_grad, ffn_out_grad, ffn_bias_grad, gains_grad, shifts_grad = (
        lax.psum(qkv_own.astype(jnp.bfloat16), "dp").astype(jnp.float32),
        lax.psum(out_own.astype(jnp.bfloat16), "dp").astype(jnp.float32),
        lax.psum(ffn_in_own.astype(jnp.bfloat16), "dp").astype(jnp.float32),
        lax.psum(ffn_out_own.astype(jnp.bfloat16), "dp").astype(jnp.float32),
        lax.psum(bias_own.astype(jnp.bfloat16), "dp").astype(jnp.float32),
        lax.psum(gains_own.astype(jnp.bfloat16), "dp").astype(jnp.float32),
        lax.psum(shifts_own.astype(jnp.bfloat16), "dp").astype(jnp.float32),
    )
    return (
        layer_out,
        frames_grad,
        qkv_grad,
        out_grad,
        ffn_in_grad,
        ffn_out_grad,
        ffn_bias_grad,
        gains_grad,
        shifts_grad,
    )


def solution(mesh):
    placed = (
        P(("group", "dp"), None),
        P(("group", "dp"), None),
        P(("group", "dp")),
        P("group"),
        P("group"),
        P("group"),
        P("group", None),
        P("group", None),
        P("group", None),
        P("group", None),
        P("group", None),
        P("group", None),
        P("group", None),
        P(("group", "dp"), None),
    )
    return jax.shard_map(
        on_device,
        mesh=mesh,
        in_specs=placed,
        out_specs=(
            P(("group", "dp"), None),
            P(("group", "dp"), None),
            P("group", None),
            P("group", None),
            P("group", None),
            P("group", None),
            P("group", None),
            P("group", None),
            P("group", None),
        ),
        check_vma=False,
    )
```

profile of v0, /device:TPU:0, one launch (start us, length us, event | category | flops | bytes accessed | tf_op | source)
XLA Modules:
  0.0 937.6 jit_solution(7582700100048097039)
XLA Ops:
  22.4 36.0 %all-reduce.16 = bf16[3072]{0:T(1024)(128)(2,1)S(1)} all-reduce(bf16[3072]{0:T(1024)(128)(2,1)S(1)} %dynamic-update-slice), channel_id=1, replica_groups=mesh['group'=16,'dp'=2] {'group'}, use_global_device_ids=true, to_apply=%add.16 | all-reduce | flops 3072 | bytes 12288
  58.4 17.0 %all-gather.1 = bf16[16,48,2]{1,2,0:T(2,128)(2,1)S(1)} all-gather(bf16[1,48,2]{1,2,0:T(2,128)(2,1)S(1)} %convert_bitcast_fusion.1), channel_id=1, replica_groups=mesh['group'=16,'dp'=2] {'group'}, dimensions={0}, use_global_device_ids=true | all-gather | bytes 3264 | tf_op jit(solution)/shard_map/all_gather | solution.py:192
  77.9 19.3 %all-gather = bf16[16,48,7]{1,2,0:T(8,128)(2,1)S(1)} all-gather(bf16[1,48,7]{1,2,0:T(8,128)(2,1)S(1)} %convert_bitcast_fusion), channel_id=1, replica_groups=mesh['group'=16,'dp'=2] {'group'}, dimensions={0}, use_global_device_ids=true | all-gather | bytes 11424 | tf_op jit(solution)/shard_map/all_gather | solution.py:193
  101.9 8.9 add_convert_fusion
  110.8 6.7 copy.91
  117.7 52.4 %while.34 = (s32[]{:T(128)}, bf16[1024,768]{0,1:T(8,128)(2,1)S(1)}, f32[12,1024]{1,0:T(8,128)S(1)}, bf16[1024,2304]{0,1:T(8,128)(2,1)}, s32[1024]{0:T(1024)S(1)}...) while((s32[]{:T(128)}, bf16[1024,768]{0,1:T(8,128)(2,1)S(1)}, ...), condition=%wide.region_5.6_spmd.clone, body=%wide.region_2.5_spmd.clone.sunk | while | flops 563214336 | bytes 32575852 | solution.py:159
  121.4 2.0 fusion.138
  123.4 2.8 fusion.139
  128.2 1.9 fusion.137
  130.1 2.0 fusion.138
  132.1 2.8 fusion.139
  138.8 2.0 fusion.138
  140.8 2.8 fusion.139
  147.5 2.0 fusion.138
  149.5 2.8 fusion.139
  156.1 2.0 fusion.138
  158.1 2.8 fusion.139
  164.8 2.0 fusion.138
  166.8 2.8 fusion.139
  171.3 4.1 fusion.91
  175.9 38.7 %fusion.23 = (bf16[1024,3072]{1,0:T(8,128)(2,1)}, f32[1024,3072]{1,0:T(8,128)}) fusion(f32[3072]{0:T(1024)S(1)} %convert_select_fusion, bf16[768,3072]{1,0:T(8,128)(2,1)} %all-gather.11.cloned.1.call-done, f32[3072]{0:T(1024)S(1)} %fusion.57, f32[768]{0:T(1024)S(1)} %fusion.66, f32[768]{0:T(1024)S(1)} %fusion.64, f32[768]{0:T(1024)S(1)} %get-tuple-element.444, ...), kind=kOutput, calls=%fused_computation.43 | convolution fusion | flops 5052039168 | bytes 26780672 | tf_op jit(solution)/shard_map/dot_general | solution.py:212
  214.7 10.0 %fusion.92 = (f32[1024]{0:T(1024)S(1)}, f32[1024,768]{0,1:T(8,128)S(1)}) fusion(f32[768]{0:T(1024)S(1)} %copy-done.36, bf16[1024,3072]{1,0:T(8,128)(2,1)} %get-tuple-element.498, bf16[3072,768]{1,0:T(8,128)(2,1)} %all-gather.13.cloned.1.call-done, f32[768]{0:T(1024)S(1)} %fusion.66, f32[3072]{0:T(1024)S(1)} %fusion.57, f32[768]{0:T(1024)S(1)} %fusion.64, ...), kind=kOutput, calls=%fused_computation.193 | convolution fusion | flops 4845992960 | bytes 17338368 | tf_op jit(solution)/shard_map/dot_general | solution.py:218
  226.1 2.5 multiply_reduce_fusion.2
  228.7 3.7 convert_reduce_fusion.2
  232.3 15.1 %convert_reduce_fusion = (f32[3072]{0:T(1024)}, bf16[1024,3072]{1,0:T(8,128)(2,1)S(1)}) fusion(f32[1024,3072]{1,0:T(8,128)} %get-tuple-element.499, f32[3072]{0:T(1024)S(1)} %convert_select_fusion, bf16[3072,768]{1,0:T(8,128)(2,1)S(1)} %copy-done.40, f32[768]{0:T(1024)S(1)} %fusion.66, f32[3072]{0:T(1024)S(1)} %fusion.57, ...), kind=kOutput, calls=%fused_computation.50 | convolution fusion | flops 4880593920 | bytes 26778624 | tf_op jit(solution)/shard_map/td,fd->tf/dot_general | solution.py:231
  247.4 6.7 multiply_reduce_fusion.3
  254.2 2.0 convert_reduce_fusion.3
  257.9 2.9 fusion.76
  260.8 4.6 convolution_convert_fusion
  265.5 2.7 broadcast_in_dim.154
  268.2 109.0 %while.35 = (s32[]{:T(128)}, bf16[1024,2304]{0,1:T(8,128)(2,1)}, bf16[1024,2304]{0,1:T(8,128)(2,1)}, f32[12,1024]{1,0:T(8,128)}, bf16[1024,768]{1,0:T(8,128)(2,1...) while((s32[]{:T(128)}, bf16[1024,2304]{0,1:T(8,128)(2,1)}, ...), condition=%wide.region_16.17_spmd.clone, body=%wide.region_14.16_spmd.clone.sunk | while | flops 1375336448 | bytes 73986424 | solution.py:290
  273.8 2.5 fusion.153
  276.3 3.4 multiply_reduce_fusion.9
  279.7 2.7 multiply_convert_fusion.7
  291.9 2.5 fusion.153
  294.4 3.4 multiply_reduce_fusion.9
  297.8 2.7 multiply_convert_fusion.7
  309.9 2.5 fusion.153
  312.4 3.4 multiply_reduce_fusion.9
  315.9 2.7 multiply_convert_fusion.7
  328.0 2.5 fusion.153
  330.5 3.4 multiply_reduce_fusion.9
  334.0 2.7 multiply_convert_fusion.7
  346.1 2.5 fusion.153
  348.6 3.4 multiply_reduce_fusion.9
  352.0 2.7 multiply_convert_fusion.7
  364.2 2.5 fusion.153
  366.7 3.4 multiply_reduce_fusion.9
  370.1 2.7 multiply_convert_fusion.7
  377.2 8.5 fusion.82
  387.6 11.1 %fusion.85 = f32[768,3072]{1,0:T(8,128)} fusion(bf16[1024,3072]{1,0:T(8,128)(2,1)} %copy-done.42, f32[768]{0:T(1024)S(1)} %copy-done.35, f32[768]{0:T(1024)S(1)} %get-tuple-element.444, f32[768]{0:T(1024)S(1)} %fusion.66, f32[1024,768]{0,1:T(8,128)S(1)} %copy-done.2, f32[1024]{0:T(1024)S(1)} %add_rsqrt_fusion.1, f32[1024]{0:T(1024)S(1)} %broadcast_divide_fusion.5), kind=kOutput, calls=%fused_computation.190 | convolution fusion | flops 4837343232 | bytes 18891776 | tf_op jit(solution)/shard_map/td,tf->df/dot_general | solution.py:233
  398.8 2.1 copy-done.9
  400.9 10.7 %fusion.79 = f32[3072,768]{1,0:T(8,128)} fusion(bf16[1024,3072]{1,0:T(8,128)(2,1)} %get-tuple-element.498, f32[1024,768]{0,1:T(8,128)S(1)} %copy-done.9), kind=kOutput, calls=%fused_computation.186 | convolution fusion | flops 4832624640 | bytes 18874368 | tf_op jit(solution)/shard_map/tf,td->fd/dot_general | solution.py:230
  413.3 3.8 convert_reduce_fusion.1
  419.1 9.0 multiply_reduce_fusion.1
  430.9 42.3 %reduce-scatter.14.cloned.1.call-done = f32[48,2304]{1,0:T(8,128)} async-done(((f32[768,2304]{1,0:T(8,128)}), f32[48,2304]{1,0:T(8,128)}) %reduce-scatter.14.cloned.1.call-update) | async-done | bytes 442384 | tf_op jit(solution)/shard_map/reduce_scatter | solution.py:315
  474.8 113.3 %reduce-scatter.18.cloned.1.call-done = f32[48,3072]{1,0:T(8,128)} async-done(((f32[768,3072]{1,0:T(8,128)}), f32[48,3072]{1,0:T(8,128)}) %reduce-scatter.18.cloned.1.call-update) | async-done | bytes 589840 | tf_op jit(solution)/shard_map/reduce_scatter | solution.py:317
  589.9 114.0 %reduce-scatter.20.cloned.1.call-done = f32[192,768]{1,0:T(8,128)} async-done(((f32[3072,768]{1,0:T(8,128)}), f32[192,768]{1,0:T(8,128)}) %reduce-scatter.20.cloned.1.call-update) | async-done | bytes 589840 | tf_op jit(solution)/shard_map/reduce_scatter | solution.py:318
  707.3 3.5 copy.100
  710.8 52.5 %reduce-scatter.24.cloned.1.call-done = f32[48,2]{1,0:T(8,128)} async-done(((f32[768,2]{1,0:T(8,128)}), f32[48,2]{1,0:T(8,128)}) %reduce-scatter.24.cloned.1.call-update) | async-done | bytes 400
  764.2 61.7 %reduce-scatter.22.cloned.1.call-done = f32[192,1]{1,0:T(8,128)} async-done(((f32[3072,1]{1,0:T(8,128)}), f32[192,1]{1,0:T(8,128)}) %reduce-scatter.22.cloned.1.call-update) | async-done | bytes 784
  826.8 57.7 %reduce-scatter.26.cloned.1.call-done = f32[48,7]{1,0:T(8,128)} async-done(((f32[768,7]{1,0:T(8,128)}), f32[48,7]{1,0:T(8,128)}) %reduce-scatter.26.cloned.1.call-update) | async-done | bytes 1360
  885.3 4.9 all-reduce.17
  892.0 31.7 %all-reduce.21.cloned.1.call-done = (bf16[48,2304]{1,0:T(8,128)(2,1)}, bf16[48,768]{1,0:T(8,128)(2,1)}, bf16[48,3072]{1,0:T(8,128)(2,1)}, bf16[192,768]{1,0:T(8,128)(2,1)}) async-done(((bf16[48,2304]{1,0:T(8,128)(2,1)}, bf16[48,768]{1,0:T(8,128)(2,1)}, bf16[48,3072]{1,0:T(8,128)(2,1)}, bf16[192,768]{1,0:T(8,128)(2,1)}), (bf16[48,2304]{1,0:T(8,128)(2,1)}, bf16[48,768]{1,0:T(8,128)(2,1)}, ...) | async-done | bytes 884752 | tf_op jit(solution)/shard_map/psum | solution.py:324
  (291 shorter events, 128.2 us)
Async XLA Ops:
  7.2 91.4 %copy-start.10 = (bf16[1024,768]{1,0:T(8,128)(2,1)S(1)}, bf16[1024,768]{1,0:T(8,128)(2,1)}, u32[]{:S(2)}) copy-start(bf16[1024,768]{1,0:T(8,128)(2,1)} %param.18) | copy-start | bytes 4718596
  7.2 93.0 %copy-start.11 = (bf16[1024,768]{1,0:T(8,128)(2,1)S(1)}, bf16[1024,768]{1,0:T(8,128)(2,1)}, u32[]{:S(2)}) copy-start(bf16[1024,768]{1,0:T(8,128)(2,1)} %param.31) | copy-start | bytes 4718596
  7.2 94.7 %all-gather.7.cloned.1.call-start = ((), (), s32[]{:S(2)}) async-start(), calls=%async_computation.7 | async-start | bytes 3760128 | tf_op jit(solution)/shard_map/all_gather | solution.py:187
  9.1 160.9 %all-gather.9.cloned.1.call-start = ((), (), s32[]{:S(2)}) async-start(), calls=%async_computation.8 | async-start | bytes 1253376 | tf_op jit(solution)/shard_map/all_gather | solution.py:188
  10.8 165.1 %all-gather.11.cloned.1.call-start = ((), (), s32[]{:S(2)}) async-start(), calls=%async_computation.9 | async-start | bytes 5013504 | tf_op jit(solution)/shard_map/all_gather | solution.py:189
  12.7 202.0 %all-gather.13.cloned.1.call-start = ((), (), s32[]{:S(2)}) async-start(), calls=%async_computation.10 | async-start | bytes 5013504 | tf_op jit(solution)/shard_map/all_gather | solution.py:190
  14.5 414.8 %reduce-scatter.16.cloned.1.call-start = ((), (), s32[]{:S(2)}) async-start(), calls=%async_computation.12 | async-start | bytes 2506752 | tf_op jit(solution)/shard_map/reduce_scatter | solution.py:316
  19.6 151.6 %copy-start.23 = (f32[768]{0:T(1024)}, f32[768]{0:T(1024)S(1)}, u32[]{:S(2)}) copy-start(f32[768]{0:T(1024)S(1)} %fusion.61) | copy-start | bytes 9220
  77.9 19.3 %copy-start.21 = (f32[1024]{0:T(1024)}, f32[1024]{0:T(1024)S(1)}, u32[]{:S(2)}) copy-start(f32[1024]{0:T(1024)S(1)} %get-tuple-element.480) | copy-start | bytes 12292
  77.9 93.4 %copy-start.38 = (pred[1024]{0:T(1024)(128)(4,1)}, pred[1024]{0:T(1024)(128)(4,1)S(1)}, u32[]{:S(2)}) copy-start(pred[1024]{0:T(1024)(128)(4,1)S(1)} %broadcast_compare_fusion.2) | copy-start | bytes 3076
  77.9 32.9 %copy-start.28 = (f32[2304]{0:T(1024)}, f32[2304]{0:T(1024)S(1)}, u32[]{:S(2)}) copy-start(f32[2304]{0:T(1024)S(1)} %pad_maximum_fusion) | copy-start | bytes 27652
  97.4 73.9 %copy-start.31 = (f32[768]{0:T(1024)}, f32[768]{0:T(1024)S(1)}, u32[]{:S(2)}) copy-start(f32[768]{0:T(1024)S(1)} %get-tuple-element.443) | copy-start | bytes 9220
  98.0 116.7 %copy-start.34 = (f32[768]{0:T(1024)}, f32[768]{0:T(1024)S(1)}, u32[]{:S(2)}) copy-start(f32[768]{0:T(1024)S(1)} %fusion.64) | copy-start | bytes 9220
  170.0 0.6 copy-start.4
  170.0 1.2 copy-start.13
  170.1 1.2 copy-start.15
  175.3 78.8 %copy-start.1 = (f32[1024,768]{0,1:T(8,128)}, f32[1024,768]{0,1:T(8,128)S(1)}, u32[]{:S(2)}) copy-start(f32[1024,768]{0,1:T(8,128)S(1)} %get-tuple-element.497) | copy-start | bytes 9437188
  175.9 38.8 %copy-start.36 = (f32[768]{0:T(1024)S(1)}, f32[768]{0:T(1024)}, u32[]{:S(2)}) copy-start(f32[768]{0:T(1024)} %fusion.63) | copy-start | bytes 9220
  214.7 10.6 %copy-start.16 = (f32[768]{0:T(1024)S(1)}, f32[768]{0:T(1024)}, u32[]{:S(2)}) copy-start(f32[768]{0:T(1024)} %get-tuple-element.445) | copy-start | bytes 9220
  214.7 10.6 %copy-start.17 = (f32[1024]{0:T(1024)S(1)}, f32[1024]{0:T(1024)}, u32[]{:S(2)}) copy-start(f32[1024]{0:T(1024)} %convert_convert_fusion) | copy-start | bytes 12292
  224.7 1.4 copy-start
  224.7 3.9 copy-start.20
  228.6 3.7 copy-start.40
  228.6 18.8 %slice-start = ((s8[4718592]{0:T(1024)(128)(4,1)}), s8[4194304]{0:T(1024)(128)(4,1)S(1)}, s32[]{:S(2)}) async-start(s8[4718592]{0:T(1024)(128)(4,1)} %bitcast.156), calls=%async_computation.19 | async-start | bytes 8388608
  232.3 15.1 %copy-start.8 = (f32[1024,768]{0,1:T(8,128)}, f32[1024,768]{0,1:T(8,128)S(1)}, u32[]{:S(2)}) copy-start(f32[1024,768]{0,1:T(8,128)S(1)} %get-tuple-element.476) | copy-start | bytes 9437188
  232.3 15.1 %slice-start.1 = ((s8[4718592]{0:T(1024)(128)(4,1)}), s8[524288]{0:T(1024)(128)(4,1)S(1)}, s32[]{:S(2)}) async-start(s8[4718592]{0:T(1024)(128)(4,1)} %bitcast.156), calls=%async_computation.20 | async-start | bytes 1048576
  247.4 6.8 copy-start.42
  254.2 3.7 copy-start.14
  256.2 1.7 copy-start.6
  257.9 2.9 copy-start.24
  257.9 2.9 copy-start.41
  260.8 212.4 %reduce-scatter.14.cloned.1.call-start = ((), (), s32[]{:S(2)}) async-start(), calls=%async_computation.11 | async-start | bytes 7520256 | tf_op jit(solution)/shard_map/reduce_scatter | solution.py:315
  265.5 2.7 copy-start.5
  268.2 109.0 %copy-start.12 = (bf16[1024,768]{0,1:T(8,128)(2,1)S(1)}, bf16[1024,768]{0,1:T(8,128)(2,1)}, u32[]{:S(2)}) copy-start(bf16[1024,768]{0,1:T(8,128)(2,1)} %copy.90) | copy-start | bytes 4718596
  268.2 109.0 %copy-start.32 = (f32[768]{0:T(1024)S(1)}, f32[768]{0:T(1024)}, u32[]{:S(2)}) copy-start(f32[768]{0:T(1024)} %copy-done.31) | copy-start | bytes 9220
  268.2 109.1 %copy-start.39 = (pred[1024]{0:T(1024)(128)(4,1)S(1)}, pred[1024]{0:T(1024)(128)(4,1)}, u32[]{:S(2)}) copy-start(pred[1024]{0:T(1024)(128)(4,1)} %copy-done.38) | copy-start | bytes 3076
  385.7 1.9 copy-start.2
  385.7 1.9 copy-start.35
  385.8 202.3 %reduce-scatter.18.cloned.1.call-start = ((), (), s32[]{:S(2)}) async-start(), calls=%async_computation.13 | async-start | bytes 10027008 | tf_op jit(solution)/shard_map/reduce_scatter | solution.py:317
  398.7 2.2 copy-start.9
  398.7 305.2 %reduce-scatter.20.cloned.1.call-start = ((), (), s32[]{:S(2)}) async-start(), calls=%async_computation.14 | async-start | bytes 10027008 | tf_op jit(solution)/shard_map/reduce_scatter | solution.py:318
  411.7 0.7 copy-start.25
  411.7 0.7 copy-start.33
  411.7 5.5 copy-start.26
  411.7 5.6 copy-start.27
  411.7 351.6 %reduce-scatter.24.cloned.1.call-start = ((), (), s32[]{:S(2)}) async-start(), calls=%async_computation.16 | async-start | bytes 417792
  413.3 5.8 copy-start.7
  413.3 5.8 copy-start.22
  413.3 5.8 copy-start.29
  413.3 5.8 copy-start.30
  417.2 408.7 %reduce-scatter.22.cloned.1.call-start = ((), (), s32[]{:S(2)}) async-start(), calls=%async_computation.15 | async-start | bytes 1671168
  419.0 465.5 %reduce-scatter.26.cloned.1.call-start = ((), (), s32[]{:S(2)}) async-start(), calls=%async_computation.17 | async-start | bytes 417792
  419.1 9.0 copy-start.37
  419.1 9.0 copy-start.19
  419.1 9.0 copy-start.18
  428.1 277.6 %copy-start.3 = (bf16[1024,768]{0,1:T(8,128)(2,1)S(1)}, bf16[1024,768]{0,1:T(8,128)(2,1)}, u32[]{:S(2)}) copy-start(bf16[1024,768]{0,1:T(8,128)(2,1)} %get-tuple-element.491) | copy-start | bytes 4718596
  429.2 494.5 %all-reduce.21.cloned.1.call-start = ((), (), s32[]{:S(2)}) async-start(), calls=%async_computation.18 | async-start | bytes 1769472 | tf_op jit(solution)/shard_map/psum | solution.py:324
Sparse Core Ops, SparseCore 0:
  10.9 50.3 all-gather.6
  64.1 37.4 all-gather.8
  104.5 52.2 all-gather.10
  159.5 51.7 all-gather.12
  260.9 60.2 reduce-scatter.15
  385.9 87.1 reduce-scatter.13
  477.2 110.8 reduce-scatter.17
  592.8 111.0 reduce-scatter.19
  708.0 55.3 reduce-scatter.23
  767.3 58.4 reduce-scatter.21
  829.9 54.5 reduce-scatter.25
  887.6 36.0 all-reduce.20
where the time goes:
time: 955 us; the launch traced here: 938 us
  waiting for transfers between devices  473 us (50%)
  matrix products  215 us (23%)
  other arithmetic  78.3 us (8%)
  blocking collectives  77.2 us (8%)
  local copies, waits for them, and re-layouts  73.6 us (8%)
  between operations  17.7 us (2%)
    unnamed x15, waiting for transfers between devices  172 us
    reduce_scatter x1, waiting for transfers between devices, on_device(): lax.psum_scatter(ffn_out_part, 'group', scatter_dimension=0, tiled=True)  114 us
    reduce_scatter x1, waiting for transfers between devices, on_device(): lax.psum_scatter(ffn_in_part, 'group', scatter_dimension=0, tiled=True)  113 us
    reduce_scatter x1, waiting for transfers between devices, on_device(): lax.psum_scatter(qkv_part, 'group', scatter_dimension=0, tiled=True)  42.3 us
    dot_general x1, matrix products, on_device(): jnp.dot(hidden_low, in_masked, preferred_element_type=jnp.float32)  38.7 us
    unnamed x1, blocking collectives  36 us
    psum x1, waiting for transfers between devices, on_device(): lax.psum(qkv_own.astype(jnp.bfloat16), 'dp').astype(jnp.float32)  31.7 us
    unnamed x104, local copies, waits for them, and re-layouts  31.1 us
  transfers between devices with their start and end apart: 12, of which 7 were waited for; matrix products, arithmetic and copies ran while one was open for 33% of the time, Pallas kernels for 0%

commit v1 on v0

--- a/solution.py
+++ b/solution.py
@@ -1,6 +1,10 @@
+import functools
+
 import jax
 import jax.numpy as jnp
 from jax import lax
+from jax.experimental import pallas as pl
+from jax.experimental.pallas import tpu as pltpu
 from jax.sharding import PartitionSpec as P
 
 D = 768
@@ -15,6 +19,393 @@
 far_score = -1000000000.0
 root_half = 0.7071067811865476
 inv_root_tau = 0.3989422804014327
+
+
+MESH = pl.DeviceIdType.MESH
+
+
+class Place:
+    def __init__(self, depth):
+        group, dp = lax.axis_index("group"), lax.axis_index("dp")
+        self.depth = depth
+        self.group, self.dp = group, dp
+        self.z, self.x, self.c, self.y = group // 4, (group // 2) % 2, group % 2, dp % 2
+        self.core_dev = (group + 1 - 2 * self.c, dp)
+        self.x_dev = (group + 2 - 4 * self.x, dp)
+        self.y_dev = (group, dp + 1 - 2 * self.y)
+
+    def z_at(self, step):
+        return lax.rem(self.z + step, self.depth)
+
+    def z_from(self, step):
+        return lax.rem(self.z - step + self.depth, self.depth)
+
+    def z_dev(self, step):
+        return ((self.z_at(step) * 2 + self.x) * 2 + self.c, self.dp)
+
+    def greet(self):
+        barrier = pltpu.get_barrier_semaphore()
+        devs = [self.core_dev, self.x_dev, self.y_dev] + [self.z_dev(s) for s in range(1, self.depth)]
+        for dev in devs:
+            pl.semaphore_signal(barrier, inc=1, device_id=dev, device_id_type=MESH)
+        pl.semaphore_wait(barrier, len(devs))
+
+
+class Copies:
+    def __init__(self, send_sems, recv_sems):
+        self.send_sems, self.recv_sems, self.count, self.made = send_sems, recv_sems, 0, []
+
+    def to(self, src, dst, dev):
+        spot = self.count
+        self.count += 1
+        copy = pltpu.make_async_remote_copy(
+            src_ref=src, dst_ref=dst, send_sem=self.send_sems.at[spot], recv_sem=self.recv_sems.at[spot],
+            device_id=dev, device_id_type=MESH)
+        self.made.append(copy)
+        return copy
+
+    def finish(self):
+        for copy in self.made:
+            copy.wait_send()
+
+
+def halves(width, y):
+    half = width // 2
+    mine = pl.ds(pl.multiple_of(y * half, 128), half)
+    other = pl.ds(pl.multiple_of((1 - y) * half, 128), half)
+    return mine, other
+
+
+def gather_cross(here, copies, own, at, width):
+    z, x, c = here.z, here.x, here.c
+    mine, other = halves(width, here.y)
+    full = slice(None)
+    steps = range(1, here.depth)
+    first = copies.to(own(mine), at(z, x, c, mine), here.x_dev)
+    own_core = copies.to(own(full), at(z, x, c, full), here.core_dev)
+    own_z = [copies.to(own(mine), at(z, x, c, mine), here.z_dev(s)) for s in steps]
+
+    def same(zz, xx, cols, dev):
+        return copies.to(at(zz, xx, c, cols), at(zz, xx, c, cols), dev)
+
+    side_z = [same(z, 1 - x, mine, here.z_dev(s)) for s in steps]
+    spots = [(z, 1 - x)] + [(here.z_from(s), x) for s in steps] + [(here.z_from(s), 1 - x) for s in steps]
+    y_hops = [same(zz, xx, mine, here.y_dev) for zz, xx in spots]
+    core_mine = [same(zz, xx, mine, here.core_dev) for zz, xx in spots]
+    core_other = [same(zz, xx, other, here.core_dev) for zz, xx in spots]
+    n = len(own_z)
+
+    def stage0():
+        first.start()
+        for copy in own_z:
+            copy.start()
+        own_core.start()
+
+    def stage1():
+        first.wait_recv()
+        for copy in side_z:
+            copy.start()
+        y_hops[0].start()
+        core_mine[0].start()
+
+    def stage2():
+        for k in range(n):
+            own_z[k].wait_recv()
+            y_hops[1 + k].start()
+            core_mine[1 + k].start()
+
+    def stage3():
+        for k in range(n):
+            side_z[k].wait_recv()
+            y_hops[1 + n + k].start()
+            core_mine[1 + n + k].start()
+
+    def stage4():
+        for k in range(1 + 2 * n):
+            y_hops[k].wait_recv()
+            core_other[k].start()
+
+    def stage5():
+        own_core.wait_recv()
+        for copy in core_mine + core_other:
+            copy.wait_recv()
+
+    return [stage0, stage1, stage2, stage3, stage4, stage5]
+
+
+def gather_line(here, copies, own, at, width):
+    z, x, c = here.z, here.x, here.c
+    mine, other = halves(width, here.y)
+    full = slice(None)
+    steps = range(1, here.depth)
+    own_z = [copies.to(own(mine), at(z, x, c, mine), here.z_dev(s)) for s in steps]
+    own_x = copies.to(own(full), at(z, x, c, full), here.x_dev)
+    own_core = copies.to(own(full), at(z, x, c, full), here.core_dev)
+
+    def same(zz, xx, cols, dev):
+        return copies.to(at(zz, xx, c, cols), at(zz, xx, c, cols), dev)
+
+    froms = [here.z_from(s) for s in steps]
+    y_hops = [same(zz, x, mine, here.y_dev) for zz in froms]
+    x_mine = [same(zz, x, mine, here.x_dev) for zz in froms]
+    x_other = [same(zz, x, other, here.x_dev) for zz in froms]
+    core_side = same(z, 1 - x, full, here.core_dev)
+    core_mine = [same(zz, x, mine, here.core_dev) for zz in froms]
+    core_other = [same(zz, x, other, here.core_dev) for zz in froms]
+    core_x_mine = [same(zz, 1 - x, mine, here.core_dev) for zz in froms]
+    core_x_other = [same(zz, 1 - x, other, here.core_dev) for zz in froms]
+    n = len(own_z)
+
+    def stage0():
+        for copy in own_z:
+            copy.start()
+        own_x.start()
+        own_core.start()
+
+    def stage1():
+        for k in range(n):
+            own_z[k].wait_recv()
+            y_hops[k].start()
+            x_mine[k].start()
+            core_mine[k].start()
+
+    def stage2():
+        own_x.wait_recv()
+        core_side.start()
+
+    def stage3():
+        for k in range(n):
+            y_hops[k].wait_recv()
+            x_other[k].start()
+            core_other[k].start()
+
+    def stage4():
+        for k in range(n):
+            x_mine[k].wait_recv()
+            core_x_mine[k].start()
+        for k in range(n):
+            x_other[k].wait_recv()
+            core_x_other[k].start()
+
+    def stage5():
+        own_core.wait_recv()
+        core_side.wait_recv()
+        for copy in core_mine + core_other + core_x_mine + core_x_other:
+            copy.wait_recv()
+
+    return [stage0, stage1, stage2, stage3, stage4, stage5]
+
+
+def gather_copies(depth):
+    return 2 + (depth - 1) * 2 + 3 * (2 * depth - 1) + (depth - 1) * 8 + 3
+
+
+def plus(a, b):
+    return (a.astype(jnp.float32) + b.astype(jnp.float32)).astype(jnp.bfloat16)
+
+
+def reduce_part(here, copies, parts, room, final, width, cross):
+    z, x, c, depth = here.z, here.x, here.c, here.depth
+    mine, other = halves(width, here.y)
+    steps = range(1, depth)
+    if cross:
+        first, second, third, fourth, fifth = room
+        core = copies.to(parts.at[:, :, 1 - c], first, here.core_dev)
+        to_y = copies.to(first.at[:, :, :, other], second, here.y_dev)
+        to_z = [copies.to(second.at[here.z_at(s)], third.at[s - 1], here.z_dev(s)) for s in steps]
+        to_x = copies.to(fourth.at[1 - x], fifth, here.x_dev)
+        back = copies.to(final.at[:, mine], final.at[:, mine], here.y_dev)
+
+        def stage0():
+            core.start()
+
+        def stage1():
+            core.wait_recv()
+
+            @pl.loop(0, depth)
+            def _(zz):
+                for xx in range(2):
+                    first[zz, xx] = plus(parts[zz, xx, c], first[zz, xx])
+            to_y.start()
+
+        def stage2():
+            to_y.wait_recv()
+
+            @pl.loop(0, depth)
+            def _(zz):
+                for xx in range(2):
+                    second[zz, xx] = plus(first[zz, xx, :, mine], second[zz, xx])
+            for copy in to_z:
+                copy.start()
+
+        def stage3():
+            for copy in to_z:
+                copy.wait_recv()
+
+            @pl.loop(0, 2)
+            def _(xx):
+                total = second[z, xx].astype(jnp.float32)
+                for s in steps:
+                    total += third[s - 1, xx].astype(jnp.float32)
+                fourth[xx] = total.astype(jnp.bfloat16)
+            to_x.start()
+
+        def stage4():
+            to_x.wait_recv()
+            final[:, mine] = plus(fourth[x], fifth[...])
+            back.start()
+
+        def stage5():
+            back.wait_recv()
+    else:
+        first, second, third, fourth = room
+        core = copies.to(parts.at[:, :, 1 - c], first, here.core_dev)
+        to_x = copies.to(first.at[:, 1 - x], second, here.x_dev)
+        to_y = copies.to(second.at[:, :, other], third, here.y_dev)
+        to_z = [copies.to(third.at[here.z_at(s)], fourth.at[s - 1], here.z_dev(s)) for s in steps]
+        back = copies.to(final.at[:, mine], final.at[:, mine], here.y_dev)
+
+        def stage0():
+            core.start()
+
+        def stage1():
+            core.wait_recv()
+
+            @pl.loop(0, depth)
+            def _(zz):
+                for xx in range(2):
+                    first[zz, xx] = plus(parts[zz, xx, c], first[zz, xx])
+            to_x.start()
+
+        def stage2():
+            to_x.wait_recv()
+
+            @pl.loop(0, depth)
+            def _(zz):
+                second[zz] = plus(first[zz, x], second[zz])
+            to_y.start()
+
+        def stage3():
+            to_y.wait_recv()
+
+            @pl.loop(0, depth)
+            def _(zz):
+                third[zz] = plus(second[zz, :, mine], third[zz])
+            for copy in to_z:
+                copy.start()
+
+        def stage4():
+            for copy in to_z:
+                copy.wait_recv()
+            total = third[z].astype(jnp.float32)
+            for s in steps:
+                total += fourth[s - 1].astype(jnp.float32)
+            final[:, mine] = total.astype(jnp.bfloat16)
+            back.start()
+
+        def stage5():
+            back.wait_recv()
+
+    return [stage0, stage1, stage2, stage3, stage4, stage5]
+
+
+def reduce_room(depth, rows, width, cross):
+    half = width // 2
+    if cross:
+        shapes = [(depth, 2, rows, width), (depth, 2, rows, half), (depth - 1, 2, rows, half), (2, rows, half), (rows, half)]
+    else:
+        shapes = [(depth, 2, rows, width), (depth, rows, width), (depth, rows, half), (depth - 1, rows, half)]
+    return [pltpu.VMEM(shape, jnp.bfloat16) for shape in shapes]
+
+
+def reduce_copies(depth):
+    return 4 + depth - 1
+
+
+def run_stages(plans, skew=0):
+    order = []
+    for at, plan in enumerate(plans):
+        for s, stage in enumerate(plan):
+            order.append((s, at, stage))
+    for _, _, stage in sorted(order, key=lambda t: (t[0], t[1])):
+        stage()
+
+
+def gather_all(depth, head, kv, wide, down):
+    rows, drows = head.shape[0], down.shape[0]
+
+    def kernel(head_ref, kv_ref, wide_ref, down_ref, head_full, kv_full, wide_full, down_full, send, recv, local):
+        here = Place(depth)
+        z, x, c = here.z, here.x, here.c
+        copies = Copies(send, recv)
+        plans = [
+            gather_cross(here, copies, lambda cols: head_ref.at[:, cols], lambda zz, xx, cc, cols: head_full.at[zz, xx, cc, :, cols], head.shape[1]),
+            gather_line(here, copies, lambda cols: kv_ref.at[:, :, cols], lambda zz, xx, cc, cols: kv_full.at[:, zz, xx, cc, :, cols], 768),
+            gather_cross(here, copies, lambda cols: down_ref.at[:, cols], lambda zz, xx, cc, cols: down_full.at[zz, xx, cc, :, cols], 768),
+            gather_line(here, copies, lambda cols: wide_ref.at[:, :, cols], lambda zz, xx, cc, cols: wide_full.at[:, zz, xx, cc, :, cols], 768),
+        ]
+        here.greet()
+        keep = [
+            pltpu.make_async_copy(head_ref, head_full.at[z, x, c], local.at[0]),
+            pltpu.make_async_copy(kv_ref, kv_full.at[:, z, x, c], local.at[1]),
+            pltpu.make_async_copy(wide_ref, wide_full.at[:, z, x, c], local.at[2]),
+            pltpu.make_async_copy(down_ref, down_full.at[z, x, c], local.at[3]),
+        ]
+        for copy in keep:
+            copy.start()
+        run_stages(plans)
+        for copy in keep:
+            copy.wait()
+        copies.finish()
+
+    count = 2 * gather_copies(depth)
+    any_spec = pl.BlockSpec(memory_space=pl.ANY)
+    return pl.pallas_call(
+        kernel,
+        out_shape=(
+            jax.ShapeDtypeStruct((depth, 2, 2, rows, head.shape[1]), jnp.bfloat16),
+            jax.ShapeDtypeStruct((2, depth, 2, 2, rows, 768), jnp.bfloat16),
+            jax.ShapeDtypeStruct((5, depth, 2, 2, rows, 768), jnp.bfloat16),
+            jax.ShapeDtypeStruct((depth, 2, 2, drows, 768), jnp.bfloat16),
+        ),
+        in_specs=[any_spec] * 4,
+        out_specs=(any_spec,) * 4,
+        scratch_shapes=[pltpu.SemaphoreType.DMA((count,)), pltpu.SemaphoreType.DMA((count,)), pltpu.SemaphoreType.DMA((4,))],
+        compiler_params=pltpu.CompilerParams(collective_id=0, has_side_effects=True),
+        name="gather_all",
+    )(head, kv, wide, down)
+
+
+def reduce_all(depth, parts, crosses, vmem=60):
+    n = len(parts)
+    sizes = [(p.shape[3], p.shape[4]) for p in parts]
+
+    def kernel(*refs):
+        ins, outs, rest = refs[:n], refs[n:2 * n], refs[2 * n:]
+        here = Place(depth)
+        copies = Copies(rest[0], rest[1])
+        at, plans = 2, []
+        for k in range(n):
+            room = rest[at:at + (5 if crosses[k] else 4)]
+            at += len(room)
+            plans.append(reduce_part(here, copies, ins[k], room, outs[k], sizes[k][1], crosses[k]))
+        here.greet()
+        run_stages(plans)
+        copies.finish()
+
+    rooms = []
+    for (rows, width), cross in zip(sizes, crosses):
+        rooms += reduce_room(depth, rows, width, cross)
+    count = reduce_copies(depth) * n
+    return pl.pallas_call(
+        kernel,
+        out_shape=tuple(jax.ShapeDtypeStruct(s, jnp.bfloat16) for s in sizes),
+        in_specs=[pl.BlockSpec(memory_space=pltpu.VMEM)] * n,
+        out_specs=(pl.BlockSpec(memory_space=pltpu.VMEM),) * n,
+        scratch_shapes=[pltpu.SemaphoreType.DMA((count,)), pltpu.SemaphoreType.DMA((count,))] + rooms,
+        compiler_params=pltpu.CompilerParams(collective_id=1, has_side_effects=True, vmem_limit_bytes=vmem * 2**20),
+        name="reduce_all",
+    )(*parts)
 
 
 def subnet_masks(width_pick, head_pick, ffn_pick):
@@ -74,6 +465,7 @@
 
 
 def on_device(
+    dp_size,
     frames,
     lengths,
     mask_starts,
@@ -183,15 +575,30 @@
             inv_one,
         )
 
-    qkv_full, out_full, ffn_in_full, ffn_out_full, ffn_bias_full, gains_full, shifts_full = (
-        lax.all_gather(qkv_weight.astype(jnp.bfloat16), "group", axis=0, tiled=True),
-        lax.all_gather(out_weight.astype(jnp.bfloat16), "group", axis=0, tiled=True),
-        lax.all_gather(ffn_in_weight.astype(jnp.bfloat16), "group", axis=0, tiled=True),
-        lax.all_gather(ffn_out_weight.astype(jnp.bfloat16), "group", axis=0, tiled=True),
-        lax.all_gather(ffn_bias.astype(jnp.bfloat16), "group", axis=0, tiled=True),
-        lax.all_gather(norm_gains.astype(jnp.bfloat16), "group", axis=0, tiled=True),
-        lax.all_gather(shifts.astype(jnp.bfloat16), "group", axis=0, tiled=True),
-    )
+    rows = qkv_weight.shape[0]
+    groups = D // rows
+    low = jnp.bfloat16
+    small = jnp.concatenate([shifts, norm_gains, ffn_bias.reshape(4, rows).T, jnp.zeros((rows, 243), jnp.float32)], axis=1)
+    head_own = jnp.concatenate([qkv_weight[:, :D], small], axis=1).astype(low)
+    kv_own = jnp.stack([qkv_weight[:, D : 2 * D], qkv_weight[:, 2 * D :]]).astype(low)
+    wide_own = jnp.stack([out_weight] + [ffn_in_weight[:, k * D : (k + 1) * D] for k in range(4)]).astype(low)
+    down_own = ffn_out_weight.astype(low)
+    fused = rows % 16 == 0 and groups % 4 == 0 and dp_size % 2 == 0
+    if fused:
+        head_full, kv_full, wide_full, down_full = gather_all(groups // 4, head_own, kv_own, wide_own, down_own)
+    else:
+        head_full = lax.all_gather(head_own, "group", axis=0, tiled=True)
+        kv_full = lax.all_gather(kv_own, "group", axis=1, tiled=True)
+        wide_full = lax.all_gather(wide_own, "group", axis=1, tiled=True)
+        down_full = lax.all_gather(down_own, "group", axis=0, tiled=True)
+    head_full = head_full.reshape(D, D + 256)
+    kv_full, wide_full = kv_full.reshape(2, D, D), wide_full.reshape(5, D, D)
+    ffn_out_full = down_full.reshape(FF, D)
+    qkv_full = jnp.concatenate([head_full[:, :D], kv_full[0], kv_full[1]], axis=1)
+    out_full = wide_full[0]
+    ffn_in_full = jnp.concatenate([wide_full[1], wide_full[2], wide_full[3], wide_full[4]], axis=1)
+    shifts_full, gains_full = head_full[:, D : D + 7], head_full[:, D + 7 : D + 9]
+    ffn_bias_full = head_full[:, D + 9 : D + 13].reshape(groups, rows, 4).transpose(0, 2, 1).reshape(FF, 1)
     front_state = attention_part(qkv_full, out_full, gains_full, shifts_full)
     (
         start_low,
@@ -311,24 +718,25 @@
     )
     gains_part = jnp.stack([gain_one, gain_two], axis=1)
     ffn_bias_part = jnp.sum(grad_pre, axis=0, dtype=jnp.float32)[:, None]
-    qkv_own, out_own, ffn_in_own, ffn_out_own, bias_own, gains_own, shifts_own = (
-        lax.psum_scatter(qkv_part, "group", scatter_dimension=0, tiled=True),
-        lax.psum_scatter(out_part, "group", scatter_dimension=0, tiled=True),
-        lax.psum_scatter(ffn_in_part, "group", scatter_dimension=0, tiled=True),
-        lax.psum_scatter(ffn_out_part, "group", scatter_dimension=0, tiled=True),
-        lax.psum_scatter(ffn_bias_part, "group", scatter_dimension=0, tiled=True),
-        lax.psum_scatter(gains_part, "group", scatter_dimension=0, tiled=True),
-        lax.psum_scatter(shifts_part, "group", scatter_dimension=0, tiled=True),
-    )
-    qkv_grad, out_grad, ffn_in_grad, ffn_out_grad, ffn_bias_grad, gains_grad, shifts_grad = (
-        lax.psum(qkv_own.astype(jnp.bfloat16), "dp").astype(jnp.float32),
-        lax.psum(out_own.astype(jnp.bfloat16), "dp").astype(jnp.float32),
-        lax.psum(ffn_in_own.astype(jnp.bfloat16), "dp").astype(jnp.float32),
-        lax.psum(ffn_out_own.astype(jnp.bfloat16), "dp").astype(jnp.float32),
-        lax.psum(bias_own.astype(jnp.bfloat16), "dp").astype(jnp.float32),
-        lax.psum(gains_own.astype(jnp.bfloat16), "dp").astype(jnp.float32),
-        lax.psum(shifts_own.astype(jnp.bfloat16), "dp").astype(jnp.float32),
-    )
+    bias_cols = ffn_bias_part.reshape(groups, 4, rows).transpose(0, 2, 1).reshape(D, 4)
+    small_part = jnp.concatenate([shifts_part, gains_part, bias_cols, jnp.zeros((D, 243), jnp.float32)], axis=1)
+    head_part = jnp.concatenate([qkv_part[:, :D], small_part], axis=1)
+    parts = [head_part, qkv_part[:, D : 2 * D], qkv_part[:, 2 * D :], out_part]
+    parts += [ffn_in_part[:, k * D : (k + 1) * D] for k in range(4)] + [ffn_out_part]
+    if fused:
+        shaped = [p.astype(low).reshape(groups // 4, 2, 2, p.shape[0] // groups, p.shape[1]) for p in parts]
+        crosses = [True, False, False, False, True, True, False, False, False]
+        owned = reduce_all(groups // 4, shaped, crosses)
+        if dp_size > 2:
+            owned = [0.5 * lax.psum(p, "dp").astype(jnp.float32) for p in owned]
+    else:
+        owned = [lax.psum_scatter(p, "group", scatter_dimension=0, tiled=True) for p in parts]
+        owned = [lax.psum(p.astype(low), "dp") for p in owned]
+    owned = [p.astype(jnp.float32) for p in owned]
+    qkv_grad = jnp.concatenate([owned[0][:, :D], owned[1], owned[2]], axis=1)
+    out_grad, ffn_in_grad, ffn_out_grad = owned[3], jnp.concatenate(owned[4:8], axis=1), owned[8]
+    shifts_grad, gains_grad = owned[0][:, D : D + 7], owned[0][:, D + 7 : D + 9]
+    ffn_bias_grad = owned[0][:, D + 9 : D + 13].T.reshape(4 * rows, 1)
     return (
         layer_out,
         frames_grad,
@@ -360,7 +768,7 @@
         P(("group", "dp"), None),
     )
     return jax.shard_map(
-        on_device,
+        functools.partial(on_device, mesh.shape["dp"]),
         mesh=mesh,
         in_specs=placed,
         out_specs=(

time: 955 us -> 643 us (0.67)
  waiting for transfers between devices: 473 us -> 0 us
  Pallas kernels: 0 us -> 197 us
  blocking collectives: 77.2 us -> 0 us
  local copies, waits for them, and re-layouts: 73.6 us -> 113 us
  matrix products: 215 us -> 243 us
  between operations: 17.7 us -> 3.72 us
    reduce_scatter x4 -> x0, waiting for transfers between devices: 270 us -> none  [the longest x1 114 us: on_device(): lax.psum_scatter(ffn_out_part, 'group', scatter_dimension=0, tiled=True)]
    pallas_call x0 -> x2, Pallas kernels: none -> 197 us  [the longest x1 108 us: reduce_all(): pl.pallas_call(kernel, out_shape=tuple((jax.ShapeDtypeStruct(s, jnp.bfloa...]
    unnamed x15 -> x0, waiting for transfers between devices: 172 us -> none
    all_gather x2 -> x0, blocking collectives: 36.3 us -> none  [the longest x1 19.3 us: on_device(): lax.all_gather(shifts.astype(jnp.bfloat16), 'group', axis=0, tiled=True)]
    unnamed x1 -> x0, blocking collectives: 36 us -> none
    psum x1 -> x0, waiting for transfers between devices: 31.7 us -> none  [on_device(): lax.psum(qkv_own.astype(jnp.bfloat16), 'dp').astype(jnp.float32)]
    while x0 -> x36, local copies, waits for them, and re-layouts: none -> 19.3 us
    dot_general x12, matrix products: 19.2 us -> 38.5 us  [pair_scores(): jnp.einsum('qhd,khd->hqk', query_heads, key_heads, preferred_element_type...]
  transfers between devices with their start and end apart: 12 -> 0, of which waited for: 7 -> 0; matrix products, arithmetic and copies ran while one was open for 33% -> 0% of each run, Pallas kernels for 0% -> 0%
where the time goes in v1:
time: 643 us; the launch traced here: 631 us
  matrix products  243 us (38%)
  Pallas kernels  197 us (31%)
  local copies, waits for them, and re-layouts  113 us (18%)
  other arithmetic  72.6 us (11%)
    pallas_call x1, Pallas kernels, reduce_all(): pl.pallas_call(kernel, out_shape=tuple((jax.ShapeDtypeStruct(s, jnp.bfloa...  108 us
    pallas_call x1, Pallas kernels, gather_all(): pl.pallas_call(kernel, out_shape=(jax.ShapeDtypeStruct((depth, 2, 2, rows...  89.8 us
    dot_general x1, matrix products, on_device(): jnp.dot(hidden_low, in_masked, preferred_element_type=jnp.float32)  39.1 us
    dot_general x12, matrix products, pair_scores(): jnp.einsum('qhd,khd->hqk', query_heads, key_heads, preferred_element_type...  38.5 us
    dot_general x6, matrix products, pair_backward(): jnp.einsum('qhd,khd->hqk', grad_heads, value_heads, preferred_element_typ...  33.3 us
    dot_general x6, matrix products, pair_forward(): jnp.einsum('hqk,khd->qhd', weights_low, value_heads, preferred_element_ty...  30.2 us
    unnamed x106, local copies, waits for them, and re-layouts  22 us
    dynamic_slice x24, local copies, waits for them, and re-layouts, column_block(): return lax.dynamic_slice_in_dim(matrix, col_start, col_count, 1)  20.6 us

profile of v1, /device:TPU:0, one launch (start us, length us, event | category | flops | bytes accessed | tf_op | source)
XLA Modules:
  0.0 631.2 jit_solution(3055410502564566873)
XLA Ops:
  8.7 89.8 %gather_all.1 = (bf16[4,2,2,48,1024]{4,3,2,1,0:T(8,128)(2,1)}, bf16[2,4,2,2,48,768]{5,4,3,2,1,0:T(8,128)(2,1)}, bf16[5,4,2,2,48,768]{5,4,3,2,1,0:T(8,128)(2,1)}, bf16[4,2,2,192,768]{4,3,2,1,0:T(8,128)(2,1)}) custom-call(bf16[48,1024]{1,0:T(8,128)(2,1)} %concatenate.120.head_ref, bf16[2,48,768]{2,1,0:T(8,128)(2,1)} %pad_maximum_fusion.1.kv_ref, ...), custom_call_target="tpu_custom_call" | custom-call | tf_op jit(solution)/shard_map/gather_all/pallas_call | solution.py:363
  102.5 6.1 fusion.87
  112.1 9.0 %add_convert_fusion = bf16[1024,2304]{1,0:T(8,128)(2,1)} fusion(f32[2304]{0:T(1024)S(1)} %pad_maximum_fusion.3, bf16[1024,768]{0,1:T(8,128)(2,1)S(1)} %copy.115, f32[768]{0:T(1024)S(1)} %get-tuple-element.530, f32[768]{0:T(1024)S(1)} %get-tuple-element.449, pred[1024]{0:T(1024)(128)(4,1)S(1)} %broadcast_compare_fusion.2, bf16[768,768]{1,0:T(8,128)(2,1)} %bitcast.205, ...), kind=kOutput, calls=%fused_computation.67 | convolution fusion | flops 3649437696 | bytes 9856000 | tf_op jit(solution)/shard_map/dot_general | solution.py:527
  121.1 6.7 %copy.116 = bf16[1024,2304]{0,1:T(8,128)(2,1)} copy(bf16[1024,2304]{1,0:T(8,128)(2,1)} %add_convert_fusion) | data formatting | bytes 9437184
  129.2 88.4 %while.34 = (s32[]{:T(128)}, bf16[1024,768]{0,1:T(8,128)(2,1)}, f32[12,1024]{1,0:T(8,128)S(1)}, bf16[1024,2304]{0,1:T(8,128)(2,1)}, s32[1024]{0:T(1024)S(1)}, /*...) while((s32[]{:T(128)}, bf16[1024,768]{0,1:T(8,128)(2,1)}, ...), condition=%wide.region_5.6_spmd.clone, body=%wide.region_2.5_spmd.clone.sunk | while | flops 563214336 | bytes 66130304 | solution.py:551
  132.9 3.2 copy-done
  136.1 2.0 fusion.144
  138.2 5.0 fusion.145
  147.7 3.2 copy-done
  152.9 5.0 fusion.145
  162.4 3.2 copy-done
  167.6 5.0 fusion.145
  177.1 3.2 copy-done
  182.4 5.0 fusion.145
  191.9 3.2 copy-done
  197.1 5.0 fusion.145
  206.6 3.2 copy-done
  211.8 5.0 fusion.145
  218.6 3.7 fusion.92
  227.4 39.1 %fusion.23 = (bf16[1024,3072]{1,0:T(8,128)(2,1)S(1)}, f32[1024,3072]{1,0:T(8,128)}) fusion(f32[3072]{0:T(1024)S(1)} %fusion.52, bf16[768,768]{1,0:T(8,128)(2,1)} %bitcast.209, bf16[768,768]{1,0:T(8,128)(2,1)} %bitcast.211, bf16[768,768]{1,0:T(8,128)(2,1)} %bitcast.213, bf16[768,768]{1,0:T(8,128)(2,1)} %bitcast.215, f32[3072]{0:T(1024)S(1)} %fusion.53, ...), kind=kOutput, calls=%fused_computation.43 | convolution fusion | flops 5073272832 | bytes 26780672 | tf_op jit(solution)/shard_map/dot_general | solution.py:619
  266.6 5.8 fusion.38
  272.5 6.2 fusion.93
  279.2 2.6 copy.121
  281.8 5.0 multiply_reduce_fusion.1
  286.8 2.5 convert_reduce_fusion.2
  289.3 9.9 %convolution_convert_fusion = bf16[3072,768]{1,0:T(8,128)(2,1)} fusion(bf16[1024,3072]{1,0:T(8,128)(2,1)} %copy-done.45, f32[1024,768]{0,1:T(8,128)S(1)} %get-tuple-element.475), kind=kOutput, calls=%fused_computation.69 | convolution fusion | flops 4834983936 | bytes 14155776 | tf_op jit(solution)/shard_map/tf,td->fd/dot_general | solution.py:637
  299.2 12.6 %fusion.94 = (bf16[3072]{0:T(1024)(128)(2,1)}, bf16[1024,3072]{1,0:T(8,128)(2,1)S(1)}) fusion(f32[1024,3072]{1,0:T(8,128)} %get-tuple-element.515, f32[3072]{0:T(1024)S(1)} %fusion.52, bf16[3072,768]{1,0:T(8,128)(2,1)S(1)} %bitcast.190, f32[1024,768]{0,1:T(8,128)S(1)} %get-tuple-element.475), kind=kOutput, calls=%fused_computation.208 | convolution fusion | flops 4870370304 | bytes 26757120 | tf_op jit(solution)/shard_map/td,fd->tf/dot_general | solution.py:638
  311.8 5.8 convolution_convert_fusion.1
  317.7 2.5 fusion.88
  321.7 6.3 multiply_reduce_fusion.2
  329.5 2.5 convolution_convert_fusion.4
  331.9 2.6 convolution_convert_fusion.3
  334.6 2.7 broadcast_in_dim.158
  337.3 141.5 %while.35 = (s32[]{:T(128)}, bf16[1024,2304]{0,1:T(8,128)(2,1)}, bf16[1024,2304]{0,1:T(8,128)(2,1)}, f32[12,1024]{1,0:T(8,128)}, bf16[1024,768]{1,0:T(8,128)(2,1...) while((s32[]{:T(128)}, bf16[1024,2304]{0,1:T(8,128)(2,1)}, ...), condition=%wide.region_16.17_spmd.clone, body=%wide.region_14.16_spmd.clone.sunk | while | flops 1375336448 | bytes 99152280 | solution.py:697
  339.0 4.5 fusion.156
  346.1 5.5 multiply_reduce_fusion.9
  351.6 2.7 multiply_convert_fusion.7
  358.1 2.5 fusion.159
  362.5 4.5 fusion.156
  369.6 5.5 multiply_reduce_fusion.9
  375.1 2.7 multiply_convert_fusion.7
  381.6 2.5 fusion.159
  385.9 4.5 fusion.156
  393.0 5.5 multiply_reduce_fusion.9
  398.6 2.7 multiply_convert_fusion.7
  405.1 2.5 fusion.159
  409.5 4.5 fusion.156
  416.6 5.5 multiply_reduce_fusion.9
  422.1 2.7 multiply_convert_fusion.7
  428.6 2.5 fusion.159
  433.0 4.5 fusion.156
  440.1 5.5 multiply_reduce_fusion.9
  445.7 2.7 multiply_convert_fusion.7
  452.1 2.5 fusion.159
  456.5 4.5 fusion.156
  463.6 5.5 multiply_reduce_fusion.9
  469.2 2.7 multiply_convert_fusion.7
  475.6 2.5 fusion.159
  478.9 6.6 %convolution_convert_fusion.2 = bf16[768,2304]{1,0:T(8,128)(2,1)S(1)} fusion(bf16[1024,2304]{0,1:T(8,128)(2,1)} %get-tuple-element.317, bf16[1024,768]{0,1:T(8,128)(2,1)S(1)} %copy-done.11, f32[768]{0:T(1024)S(1)} %get-tuple-element.530, f32[768]{0:T(1024)S(1)} %copy-done.39, pred[1024]{0:T(1024)(128)(4,1)S(1)} %copy-done.43), kind=kOutput, calls=%fused_computation.71 | convolution fusion | flops 3628793856 | bytes 9837568 | tf_op jit(solution)/shard_map/td,tc->dc/dot_general | solution.py:700
  489.3 8.1 %multiply_reduce_fusion.3 = (bf16[768]{0:T(1024)(128)(2,1)S(1)}, f32[1024,768]{0,1:T(8,128)}) fusion(f32[1024]{0:T(1024)S(1)} %copy-done.29, f32[1024]{0:T(1024)S(1)} %copy-done.40, f32[1024,768]{0,1:T(8,128)S(1)} %copy-done.8, bf16[1024,2304]{0,1:T(8,128)(2,1)} %get-tuple-element.317, bf16[768,768]{1,0:T(8,128)(2,1)S(1)} %bitcast.206, ...), kind=kOutput, calls=%fused_computation.77 | convolution fusion | flops 3644718336 | bytes 14571008 | tf_op jit(solution)/shard_map/tc,dc->td/dot_general | solution.py:702
  497.7 3.0 reduce
  504.1 3.1 concatenate.134.refs_0_
  507.3 107.6 %reduce_all.1 = (bf16[48,1024]{1,0:T(8,128)(2,1)}, bf16[48,768]{1,0:T(8,128)(2,1)}, bf16[48,768]{1,0:T(8,128)(2,1)}, bf16[48,768]{1,0:T(8,128)(2,1)}, bf16[48,76...) custom-call(bf16[4,2,2,48,1024]{4,3,2,1,0:T(8,128)(2,1)} %concatenat, ...), custom_call_target="tpu_custom_call" | custom-call | tf_op jit(solution)/shard_map/reduce_all/pallas_call | solution.py:400
  625.9 3.5 copy.138
  (318 shorter events, 129.9 us)
Async XLA Ops:
  0.6 7.3 %copy-start.23 = (f32[192,768]{1,0:T(8,128)S(1)}, f32[192,768]{1,0:T(8,128)}, u32[]{:S(2)}) copy-start(f32[192,768]{1,0:T(8,128)} %param.27) | copy-start | bytes 1769476
  0.7 100.3 %copy-start.44 = (s32[1,2]{1,0:T(1,128)S(1)}, s32[1,2]{1,0:T(1,128)}, u32[]{:S(2)}) copy-start(s32[1,2]{1,0:T(1,128)} %param.19) | copy-start | bytes 28
  0.7 100.5 %copy-start.25 = (s32[1024]{0:T(1024)S(1)}, s32[1024]{0:T(1024)}, u32[]{:S(2)}) copy-start(s32[1024]{0:T(1024)} %param.20) | copy-start | bytes 12292
  2.8 5.9 copy-start.24
  100.2 118.4 %copy-start.38 = (f32[768]{0:T(1024)}, f32[768]{0:T(1024)S(1)}, u32[]{:S(2)}) copy-start(f32[768]{0:T(1024)S(1)} %get-tuple-element.449) | copy-start | bytes 9220
  101.9 116.7 %copy-start.42 = (pred[1024]{0:T(1024)(128)(4,1)}, pred[1024]{0:T(1024)(128)(4,1)S(1)}, u32[]{:S(2)}) copy-start(pred[1024]{0:T(1024)(128)(4,1)S(1)} %broadcast_compare_fusion.2) | copy-start | bytes 3076
  102.5 6.8 %copy-start.9 = (bf16[4,2,2,48,1024]{4,3,2,1,0:T(8,128)(2,1)S(1)}, bf16[4,2,2,48,1024]{4,3,2,1,0:T(8,128)(2,1)}, u32[]{:S(2)}) copy-start(bf16[4,2,2,48,1024]{4,3,2,1,0:T(8,128)(2,1)} %get-tuple-element.311) | copy-start | bytes 4718596
  110.4 10.8 %copy-start.32 = (f32[2304]{0:T(1024)}, f32[2304]{0:T(1024)S(1)}, u32[]{:S(2)}) copy-start(f32[2304]{0:T(1024)S(1)} %pad_maximum_fusion.2) | copy-start | bytes 27652
  112.1 9.0 %copy-start.10 = (bf16[1024,768]{0,1:T(8,128)(2,1)}, bf16[1024,768]{0,1:T(8,128)(2,1)S(1)}, u32[]{:S(2)}) copy-start(bf16[1024,768]{0,1:T(8,128)(2,1)S(1)} %copy.115) | copy-start | bytes 4718596
  132.9 3.2 copy-start
  147.7 3.2 copy-start
  162.4 3.2 copy-start
  177.1 3.2 copy-start
  191.8 3.2 copy-start
  206.6 3.2 copy-start
  217.6 1.0 copy-start.26
  217.9 4.3 copy-start.20
  222.3 44.3 %copy-start.2 = (f32[1024,768]{0,1:T(8,128)}, f32[1024,768]{0,1:T(8,128)S(1)}, u32[]{:S(2)}) copy-start(f32[1024,768]{0,1:T(8,128)S(1)} %get-tuple-element.513) | copy-start | bytes 9437188
  266.5 5.9 copy-start.45
  266.6 5.8 copy-start.30
  266.6 5.8 copy-start.31
  266.6 5.9 copy-start.3
  266.6 5.9 copy-start.41
  272.4 6.3 copy-start.6
  281.8 5.0 copy-start.1
  286.8 12.4 %slice-start.2 = ((s8[4718592]{0:T(1024)(128)(4,1)}), s8[4194304]{0:T(1024)(128)(4,1)S(1)}, s32[]{:S(2)}) async-start(s8[4718592]{0:T(1024)(128)(4,1)} %bitcast.189), calls=%async_computation.2 | async-start | bytes 8388608
  289.3 9.9 %slice-start.3 = ((s8[4718592]{0:T(1024)(128)(4,1)}), s8[524288]{0:T(1024)(128)(4,1)S(1)}, s32[]{:S(2)}) async-start(s8[4718592]{0:T(1024)(128)(4,1)} %bitcast.189), calls=%async_computation.3 | async-start | bytes 1048576
  299.2 12.6 %copy-start.4 = (f32[1024,768]{0,1:T(8,128)S(1)}, f32[1024,768]{0,1:T(8,128)}, u32[]{:S(2)}) copy-start(f32[1024,768]{0,1:T(8,128)} %copy-done.2) | copy-start | bytes 9437188
  317.6 2.5 copy-start.15
  317.6 3.0 copy-start.16
  317.7 3.7 copy-start.17
  317.7 4.0 copy-start.18
  328.0 1.5 copy-start.12
  329.4 2.5 copy-start.7
  329.4 2.5 copy-start.21
  337.3 141.5 %copy-start.11 = (bf16[1024,768]{0,1:T(8,128)(2,1)S(1)}, bf16[1024,768]{0,1:T(8,128)(2,1)}, u32[]{:S(2)}) copy-start(bf16[1024,768]{0,1:T(8,128)(2,1)} %copy-done.10) | copy-start | bytes 4718596
  337.3 141.5 %copy-start.39 = (f32[768]{0:T(1024)S(1)}, f32[768]{0:T(1024)}, u32[]{:S(2)}) copy-start(f32[768]{0:T(1024)} %copy-done.38) | copy-start | bytes 9220
  337.3 141.5 %copy-start.43 = (pred[1024]{0:T(1024)(128)(4,1)S(1)}, pred[1024]{0:T(1024)(128)(4,1)}, u32[]{:S(2)}) copy-start(pred[1024]{0:T(1024)(128)(4,1)} %copy-done.42) | copy-start | bytes 3076
  345.4 6.2 slice-start
  346.0 5.6 slice-start.1
  368.9 6.2 slice-start
  369.5 5.6 slice-start.1
  392.4 6.2 slice-start
  393.0 5.6 slice-start.1
  415.9 6.2 slice-start
  416.5 5.6 slice-start.1
  439.4 6.2 slice-start
  440.1 5.6 slice-start.1
  462.9 6.2 slice-start
  463.6 5.6 slice-start.1
  485.5 2.7 copy-start.8
  485.5 3.1 copy-start.13
  485.5 3.4 copy-start.14
  485.5 3.7 copy-start.19
  485.5 3.7 copy-start.29
  485.5 3.7 copy-start.33
  485.5 3.7 copy-start.40
  497.4 5.3 copy-start.37
  497.4 5.6 copy-start.36
  497.4 5.9 copy-start.35
  497.7 6.0 copy-start.34
  614.8 9.1 %copy-start.27 = (bf16[48,768]{1,0:T(8,128)(2,1)S(1)}, bf16[48,768]{1,0:T(8,128)(2,1)}, u32[]{:S(2)}) copy-start(bf16[48,768]{1,0:T(8,128)(2,1)} %get-tuple-element.321) | copy-start | bytes 221188
  614.8 9.7 %copy-start.22 = (bf16[48,1024]{1,0:T(8,128)(2,1)S(1)}, bf16[48,1024]{1,0:T(8,128)(2,1)}, u32[]{:S(2)}) copy-start(bf16[48,1024]{1,0:T(8,128)(2,1)} %get-tuple-element.318) | copy-start | bytes 294916
  622.0 7.5 %copy-start.5 = (bf16[1024,768]{0,1:T(8,128)(2,1)S(1)}, bf16[1024,768]{0,1:T(8,128)(2,1)}, u32[]{:S(2)}) copy-start(bf16[1024,768]{0,1:T(8,128)(2,1)} %get-tuple-element.502) | copy-start | bytes 4718596
  (1 other events, 0.6 us)
